TPU v7x, 128 devices: a whole 4x4x4 slice. The times are simulated.
128 devices in a mesh: head: 4 (over x), seq: 32 (over y, z, core).
Axes of the slice: x: 4, y: 4, z: 4, core: 2. Of those that a mesh axis runs over, the one named last changes fastest.
Arguments:
- queries: bfloat16 [16384, 8192], P('seq', 'head'), may hold values from -200 to 200
- keys: bfloat16 [16384, 8192], P('seq', 'head'), may hold values from -6 to 6
- values: bfloat16 [16384, 8192], P('seq', 'head'), may hold values from -6 to 6
- cotangent: bfloat16 [16384, 8192], P('seq', 'head'), may hold values from -6 to 6
- prefix_keys: bfloat16 [16384, 8192], P('seq', 'head'), may hold values from -1.5 to 1.5
- prefix_values: bfloat16 [16384, 8192], P('seq', 'head'), may hold values from -1.5 to 1.5
- gain: float32 [8192], P('head'), may hold values from 0.5 to 1.5
- lengths: int32 [32], P('seq'), may hold values from 64 to 512, as said below
Outputs:
- normed: bfloat16 [16384, 8192], P('seq', 'head')
- query_grad: bfloat16 [16384, 8192], P('seq', 'head')
- key_grad: bfloat16 [16384, 8192], P('seq', 'head')
- value_grad: bfloat16 [16384, 8192], P('seq', 'head')
- prefix_key_grad: bfloat16 [16384, 8192], P('seq', 'head')
- prefix_value_grad: bfloat16 [16384, 8192], P('seq', 'head')
Inputs may be any that keep to these rules, and one draw needn't show every extreme that they name: `lengths`: one length per response; some response has exactly 512 live slots and some exactly 64.
All inputs are finite; a program needn't handle non-finite values.
Results may differ from a plain program's by a relative error of at most 0.0058.
Values sent between devices are 32-bit elements; how exact they have to be, the bound alone decides.
No kernel may reach another device: no remote copies, remote signals or barrier semaphores. Data moves between devices by JAX's collectives and lax.ppermute only.
A program may use at most 128 MiB of HBM per device.

v0:
```python
import functools
import jax
import jax.numpy as jnp
from jax import lax
from jax.sharding import PartitionSpec as P

H = 64
HEAD_DIM = 128
BLOCK = 256
epsilon = 1e-06


def summed_prefix(partial_state):
    return lax.psum(partial_state, "seq")


def body(queries, keys, values, cotangent, prefix_keys, prefix_values, gain, lengths):
    tok_rows, tok_cols = queries.shape
    heads_here = tok_cols // HEAD_DIM
    block_count = tok_rows // BLOCK
    length = lengths[0]
    is_live = lax.iota(jnp.int32, tok_rows) < length
    live_mask = is_live.astype(jnp.bfloat16)[:, None]
    block_shape = (block_count, BLOCK, heads_here, HEAD_DIM)
    q_live = (queries * live_mask).reshape(block_shape)
    k_live = (keys * live_mask).reshape(block_shape)
    v_live = (values * live_mask).reshape(block_shape)
    causal = (lax.iota(jnp.int32, BLOCK)[:, None] >= lax.iota(jnp.int32, BLOCK)[None, :]).astype(
        jnp.float32
    )
    pre_keys = prefix_keys.reshape(-1, heads_here, HEAD_DIM)
    pre_values = prefix_values.reshape(-1, heads_here, HEAD_DIM)
    partial_state = jnp.einsum(
        "thd,the->hde", pre_keys, pre_values, preferred_element_type=jnp.float32
    )

    def intra_block(index):
        q_block = q_live[index]
        k_block = k_live[index]
        v_block = v_live[index]
        scores = jnp.einsum("bhd,shd->hbs", q_block, k_block, preferred_element_type=jnp.float32)
        scores = (scores * causal).astype(jnp.bfloat16)
        in_block = jnp.einsum("hbs,she->bhe", scores, v_block, preferred_element_type=jnp.float32)
        block_kv = jnp.einsum("bhd,bhe->hde", k_block, v_block, preferred_element_type=jnp.float32)
        return (in_block, scores, block_kv)

    def from_state_of(index, state_bf):
        return jnp.einsum(
            "bhd,hde->bhe", q_live[index], state_bf, preferred_element_type=jnp.float32
        )

    results = []
    score_list = []
    state_list = []
    prefix_state = summed_prefix(partial_state)

    def forward_block(index, state_now):
        state_bf = state_now.astype(jnp.bfloat16)
        in_block, scores, block_kv = intra_block(index)
        return (from_state_of(index, state_bf) + in_block, scores, state_bf, state_now + block_kv)

    state_now = prefix_state
    for index in range(block_count):
        step_fn = functools.partial(forward_block, index)
        packed = step_fn(state_now)
        results.append(packed[0])
        score_list.append(packed[1])
        state_list.append(packed[2])
        state_now = packed[3]
    attended = jnp.concatenate(results, axis=0).reshape(tok_rows, tok_cols)
    scaled_cot = gain * (cotangent * live_mask).astype(jnp.float32)
    square_sum, inner_sum = lax.psum(
        (jnp.sum(attended * attended, axis=1), jnp.sum(scaled_cot * attended, axis=1)), "head"
    )
    root_mean = jnp.sqrt(square_sum / (H * HEAD_DIM) + epsilon)[:, None]
    inner_sum = inner_sum[:, None]
    normed = (gain * attended / root_mean).astype(jnp.bfloat16)
    out_grad = scaled_cot / root_mean - attended * inner_sum / (H * HEAD_DIM * root_mean**3)
    out_grad = out_grad.astype(jnp.bfloat16).reshape(block_shape)

    def backward_block(index, grad_state):
        q_block = q_live[index]
        k_block = k_live[index]
        v_block = v_live[index]
        d_block = out_grad[index]
        scores = score_list[index]
        state_bf = state_list[index]
        grad_bf = grad_state.astype(jnp.bfloat16)
        pscore = jnp.einsum("bhe,she->hbs", d_block, v_block, preferred_element_type=jnp.float32)
        pscore = (pscore * causal).astype(jnp.bfloat16)
        grad_q = jnp.einsum(
            "bhe,hde->bhd", d_block, state_bf, preferred_element_type=jnp.float32
        ) + jnp.einsum("hbs,shd->bhd", pscore, k_block, preferred_element_type=jnp.float32)
        grad_k = jnp.einsum(
            "bhe,hde->bhd", v_block, grad_bf, preferred_element_type=jnp.float32
        ) + jnp.einsum("hbs,bhd->shd", pscore, q_block, preferred_element_type=jnp.float32)
        grad_v = jnp.einsum(
            "bhd,hde->bhe", k_block, grad_bf, preferred_element_type=jnp.float32
        ) + jnp.einsum("hbs,bhe->she", scores, d_block, preferred_element_type=jnp.float32)
        grad_next = grad_state + jnp.einsum(
            "bhd,bhe->hde", q_block, d_block, preferred_element_type=jnp.float32
        )
        return (
            grad_q.astype(jnp.bfloat16),
            grad_k.astype(jnp.bfloat16),
            grad_v.astype(jnp.bfloat16),
            grad_next,
        )

    grad_state = jnp.zeros((heads_here, HEAD_DIM, HEAD_DIM), jnp.float32)
    query_parts = []
    key_parts = []
    value_parts = []
    for index in reversed(range(block_count)):
        step_fn = functools.partial(backward_block, index)
        packed = step_fn(grad_state)
        query_parts.insert(0, packed[0])
        key_parts.insert(0, packed[1])
        value_parts.insert(0, packed[2])
        grad_state = packed[3]
    total_grad = lax.psum(grad_state, "seq")
    wide_keys = pre_keys.astype(jnp.float32)
    wide_values = pre_values.astype(jnp.float32)
    prefix_key_grad = jnp.einsum(
        "the,hde->thd", wide_values, total_grad, precision=lax.Precision.HIGHEST
    )
    prefix_value_grad = jnp.einsum(
        "thd,hde->the", wide_keys, total_grad, precision=lax.Precision.HIGHEST
    )
    query_grad = jnp.concatenate(query_parts, axis=0).reshape(tok_rows, tok_cols)
    key_grad = jnp.concatenate(key_parts, axis=0).reshape(tok_rows, tok_cols)
    value_grad = jnp.concatenate(value_parts, axis=0).reshape(tok_rows, tok_cols)
    return (
        normed,
        query_grad,
        key_grad,
        value_grad,
        prefix_key_grad.astype(jnp.bfloat16).reshape(prefix_keys.shape),
        prefix_value_grad.astype(jnp.bfloat16).reshape(prefix_values.shape),
    )


def solution(mesh):
    return jax.shard_map(
        body,
        mesh=mesh,
        in_specs=(
            P("seq", "head"),
            P("seq", "head"),
            P("seq", "head"),
            P("seq", "head"),
            P("seq", "head"),
            P("seq", "head"),
            P("head"),
            P("seq"),
        ),
        out_specs=(
            P("seq", "head"),
            P("seq", "head"),
            P("seq", "head"),
            P("seq", "head"),
            P("seq", "head"),
            P("seq", "head"),
        ),
        check_vma=False,
    )
```

profile of v0, /device:TPU:1, one launch (start us, length us, event | category | flops | bytes accessed | tf_op | source)
XLA Modules:
  0.0 292.5 jit_solution(10290730926463739367)
XLA Ops:
  7.2 1.5 copy-done
  8.8 3.4 %fusion.8 = f32[16,128,128]{2,1,0:T(8,128)} fusion(bf16[512,2048]{1,0:T(8,128)(2,1)} %param.13, bf16[512,2048]{1,0:T(8,128)(2,1)S(1)} %copy-done), kind=kOutput, calls=%fused_computation.18 | convolution fusion | flops 268435456 | bytes 5242880 | tf_op jit(solution)/shard_map/thd,the->hde/dot_general | solution.py:33
  13.0 3.9 %copy.49 = bf16[512,2048]{0,1:T(8,128)(2,1)} copy(bf16[512,2048]{1,0:T(8,128)(2,1)} %param.8) | data formatting | bytes 4194304 | tf_op args[0]
  16.9 3.9 %copy.53 = bf16[512,2048]{0,1:T(8,128)(2,1)} copy(bf16[512,2048]{1,0:T(8,128)(2,1)} %param.9) | data formatting | bytes 4194304 | tf_op args[1]
  20.8 3.9 %copy.52 = bf16[512,2048]{0,1:T(8,128)(2,1)} copy(bf16[512,2048]{1,0:T(8,128)(2,1)} %param.10) | data formatting | bytes 4194304 | tf_op args[2]
  24.7 3.3 %broadcast_multiply_fusion = (bf16[512,2048]{0,1:T(8,128)(2,1)S(1)}, bf16[512,2048]{0,1:T(8,128)(2,1)S(1)}, bf16[512,2048]{0,1:T(8,128)(2,1)S(1)}) fusion(bf16[512,2048]{0,1:T(8,128)(2,1)} %copy.53, bf16[512]{0:T(512)(128)(2,1)S(1)} %fusion.38, bf16[512,2048]{0,1:T(8,128)(2,1)} %copy.52, bf16[512,2048]{0,1:T(8,128)(2,1)} %copy.49), kind=kLoop, calls=%fused_computation.49 | loop fusion | flops 3145728 | bytes 12583936 | tf_op jit(solution)/shard_map/mul | solution.py:26
  30.8 2.2 fusion.45
  33.0 2.1 multiply_convert_fusion.2
  35.1 3.9 %copy.61 = bf16[512,2048]{0,1:T(8,128)(2,1)} copy(bf16[512,2048]{1,0:T(8,128)(2,1)} %param.11) | data formatting | bytes 4194304 | tf_op args[3]
  39.0 4.1 %fusion.46 = f32[16,128,256]{2,1,0:T(8,128)} fusion(bf16[256,16,128]{0,2,1:T(8,128)(2,1)} %bitcast.148, bf16[16,256,256]{2,1,0:T(8,128)(2,1)} %multiply_convert_fusion.2), kind=kOutput, calls=%fused_computation.72 | convolution fusion | flops 268435456 | bytes 5242880 | tf_op jit(solution)/shard_map/hbs,she->bhe/dot_general | solution.py:43
  43.0 77.5 %all-reduce.4.cloned.1.call-done = f32[16,128,128]{2,1,0:T(8,128)} async-done(((f32[16,128,128]{2,1,0:T(8,128)}), f32[16,128,128]{2,1,0:T(8,128)}) %all-reduce.4.cloned.1.call-update) | async-done | bytes 1048592 | tf_op jit(solution)/shard_map/psum | solution.py:14
  120.5 2.1 fusion.29
  128.5 8.7 %all-reduce = (f32[512]{0:T(512)S(1)}, f32[512]{0:T(512)S(1)}) all-reduce(f32[512]{0:T(512)S(1)} %get-tuple-element.22, f32[512]{0:T(512)S(1)} %fusion.2), channel_id=1, replica_groups=mesh['head'=4,'seq'=32] {'head'}, use_global_device_ids=true, to_apply=%region_2.0 | all-reduce | flops 1024 | bytes 8192 | tf_op jit(solution)/shard_map/psum | solution.py:72
  137.3 4.5 %fusion.5 = (bf16[512,2048]{0,1:T(8,128)(2,1)S(1)}, bf16[512,2048]{0,1:T(8,128)(2,1)}) fusion(f32[512,16,128]{0,2,1:T(8,128)} %copy-done.1, f32[512]{0:T(512)S(1)} %get-tuple-element.32, f32[512]{0:T(512)S(1)} %get-tuple-element.19, f32[512]{0:T(512)S(1)} %get-tuple-element.33, f32[2048]{0:T(1024)S(1)} %copy-done.35, bf16[512,2048]{0,1:T(8,128)(2,1)} %copy.61, ...), kind=kLoop, calls=%fused_computation.9 | loop fusion | flops 11534336 | bytes 10501120 | tf_op jit(solution)/shard_map/convert_element_type | solution.py:79
  141.9 2.2 copy-done.18
  147.4 1.8 fusion.51
  149.1 2.1 fusion.48
  151.3 1.8 fusion.52
  154.3 1.8 fusion.50
  156.1 2.1 fusion.47
  161.1 3.4 %fusion.27 = bf16[256,16,128]{0,2,1:T(8,128)(2,1)} fusion(f32[16,128,256]{2,1,0:T(8,128)} %fusion.52, bf16[256,16,128]{0,2,1:T(8,128)(2,1)S(1)} %bitcast.124, f32[16,128,128]{2,1,0:T(8,128)} %copy-done.19), kind=kOutput, calls=%fused_computation.44 | convolution fusion | flops 135528448 | bytes 5242880 | tf_op jit(solution)/shard_map/bhd,hde->bhe/dot_general | solution.py:97
  164.5 3.6 %fusion.26 = bf16[256,16,128]{0,2,1:T(8,128)(2,1)} fusion(f32[16,128,256]{2,1,0:T(8,128)} %fusion.51, bf16[256,16,128]{0,2,1:T(8,128)(2,1)} %bitcast.149), kind=kOutput, calls=%fused_computation.43 | convolution fusion | flops 135266304 | bytes 4194304 | tf_op jit(solution)/shard_map/bhe,hde->bhd/dot_general | solution.py:94
  174.6 3.9 %copy.82 = bf16[512,2048]{1,0:T(8,128)(2,1)} copy(bf16[512,2048]{0,1:T(8,128)(2,1)} %bitcast.151) | data formatting | bytes 4194304
  178.6 4.0 %copy.80 = bf16[512,2048]{1,0:T(8,128)(2,1)} copy(bf16[512,2048]{0,1:T(8,128)(2,1)} %bitcast.152) | data formatting | bytes 4194304
  182.6 2.4 fusion.25
  186.6 3.9 %copy.81 = bf16[512,2048]{1,0:T(8,128)(2,1)} copy(bf16[512,2048]{0,1:T(8,128)(2,1)} %bitcast.153) | data formatting | bytes 4194304
  190.5 3.9 %copy.79 = bf16[512,2048]{1,0:T(8,128)(2,1)} copy(bf16[512,2048]{0,1:T(8,128)(2,1)} %get-tuple-element.21) | data formatting | bytes 4194304
  194.4 74.1 %all-reduce.6.cloned.1.call-done = f32[16,128,128]{2,1,0:T(8,128)} async-done(((f32[16,128,128]{2,1,0:T(8,128)}), f32[16,128,128]{2,1,0:T(8,128)}) %all-reduce.6.cloned.1.call-update) | async-done | bytes 1048592 | tf_op jit(solution)/shard_map/psum | solution.py:121
  268.5 4.4 %fusion.13 = bf16[16,128,512]{2,1,0:T(8,128)(2,1)} fusion(f32[16,128,128]{2,1,0:T(8,128)} %all-reduce.6.cloned.1.call-done, bf16[512,2048]{1,0:T(8,128)(2,1)S(1)} %copy-done), kind=kOutput, calls=%fused_computation.34 | convolution fusion | flops 1611661312 | bytes 5242880 | tf_op jit(solution)/shard_map/thd,hde->the/dot_general | solution.py:127
  273.0 4.0 %copy.84 = bf16[512,2048]{1,0:T(8,128)(2,1)} copy(bf16[512,2048]{0,1:T(8,128)(2,1)} %bitcast.155) | data formatting | bytes 4194304
  277.0 4.8 %fusion.16 = bf16[16,128,512]{2,1,0:T(8,128)(2,1)} fusion(f32[16,128,128]{2,1,0:T(8,128)S(1)} %copy-done.31, bf16[512,2048]{1,0:T(8,128)(2,1)} %param.13), kind=kOutput, calls=%fused_computation.35 | convolution fusion | flops 1611661312 | bytes 5242880 | tf_op jit(solution)/shard_map/the,hde->thd/dot_general | solution.py:124
  281.7 3.9 %copy.83 = bf16[512,2048]{1,0:T(8,128)(2,1)} copy(bf16[512,2048]{0,1:T(8,128)(2,1)} %bitcast.154) | data formatting | bytes 4194304
  (96 shorter events, 24.3 us)
Async XLA Ops:
  7.2 1.6 copy-start
  7.2 113.3 %all-reduce.4.cloned.1.call-start = ((), (), s32[]{:S(2)}) async-start(), calls=%async_computation | async-start | bytes 2097152 | tf_op jit(solution)/shard_map/psum | solution.py:14
  12.2 256.3 %all-reduce.6.cloned.1.call-start = ((), (), s32[]{:S(2)}) async-start(), calls=%async_computation.1 | async-start | bytes 2097152 | tf_op jit(solution)/shard_map/psum | solution.py:121
  28.1 4.8 %copy-start.20 = (bf16[256,2048]{0,1:T(8,128)(2,1)}, bf16[256,2048]{0,1:T(8,128)(2,1)S(1)}, u32[]{:S(2)}) copy-start(bf16[256,2048]{0,1:T(8,128)(2,1)S(1)} %get-tuple-element.31) | copy-start | bytes 3145732
  29.4 1.4 copy-start.2
  29.4 3.5 %copy-start.9 = (bf16[256,2048]{0,1:T(8,128)(2,1)}, bf16[256,2048]{0,1:T(8,128)(2,1)S(1)}, u32[]{:S(2)}) copy-start(bf16[256,2048]{0,1:T(8,128)(2,1)S(1)} %get-tuple-element.27) | copy-start | bytes 3145732
  30.4 2.5 copy-start.16
  120.5 2.1 copy-start.10
  120.5 2.5 copy-start.28
  123.1 1.4 copy-start.13
  123.1 1.7 copy-start.23
  123.1 2.4 copy-start.25
  126.0 1.7 copy-start.15
  126.0 1.7 copy-start.35
  126.5 2.0 copy-start.1
  141.8 2.3 copy-start.18
  141.9 3.9 %copy-start.7 = (bf16[256,2048]{0,1:T(8,128)(2,1)}, bf16[256,2048]{0,1:T(8,128)(2,1)S(1)}, u32[]{:S(2)}) copy-start(bf16[256,2048]{0,1:T(8,128)(2,1)S(1)} %get-tuple-element.25) | copy-start | bytes 3145732
  141.9 17.7 %copy-start.5 = (bf16[256,2048]{0,1:T(8,128)(2,1)}, bf16[256,2048]{0,1:T(8,128)(2,1)S(1)}, u32[]{:S(2)}) copy-start(bf16[256,2048]{0,1:T(8,128)(2,1)S(1)} %get-tuple-element.24) | copy-start | bytes 3145732
  146.6 13.1 %copy-start.19 = (f32[16,128,128]{2,1,0:T(8,128)}, f32[16,128,128]{2,1,0:T(8,128)S(1)}, u32[]{:S(2)}) copy-start(f32[16,128,128]{2,1,0:T(8,128)S(1)} %fusion.49) | copy-start | bytes 3145732
  147.3 1.8 copy-start.21
  149.1 2.1 copy-start.17
  151.3 1.8 copy-start.3
  164.5 3.6 %copy-start.8 = (bf16[256,2048]{0,1:T(8,128)(2,1)S(1)}, bf16[256,2048]{0,1:T(8,128)(2,1)}, u32[]{:S(2)}) copy-start(bf16[256,2048]{0,1:T(8,128)(2,1)} %copy-done.7) | copy-start | bytes 3145732
  164.5 3.6 %copy-start.26 = (f32[16,128,256]{2,1,0:T(8,128)S(1)}, f32[16,128,256]{2,1,0:T(8,128)}, u32[]{:S(2)}) copy-start(f32[16,128,256]{2,1,0:T(8,128)} %fusion.48) | copy-start | bytes 6291460
  164.5 3.6 %copy-start.30 = (bf16[16,128,128]{2,1,0:T(8,128)(2,1)S(1)}, bf16[16,128,128]{2,1,0:T(8,128)(2,1)}, u32[]{:S(2)}) copy-start(bf16[16,128,128]{2,1,0:T(8,128)(2,1)} %copy-done.29) | copy-start | bytes 1572868
  168.1 1.5 copy-start.34
  169.6 1.5 copy-start.6
  169.6 2.3 copy-start.24
  169.6 3.1 %copy-start.27 = (f32[16,128,256]{2,1,0:T(8,128)S(1)}, f32[16,128,256]{2,1,0:T(8,128)}, u32[]{:S(2)}) copy-start(f32[16,128,256]{2,1,0:T(8,128)} %fusion.47) | copy-start | bytes 6291460
  178.6 4.0 %copy-start.4 = (bf16[256,2048]{0,1:T(8,128)(2,1)S(1)}, bf16[256,2048]{0,1:T(8,128)(2,1)}, u32[]{:S(2)}) copy-start(bf16[256,2048]{0,1:T(8,128)(2,1)} %copy-done.2) | copy-start | bytes 3145732
  182.6 2.5 copy-start.33
  272.9 4.0 %copy-start.31 = (f32[16,128,128]{2,1,0:T(8,128)S(1)}, f32[16,128,128]{2,1,0:T(8,128)}, u32[]{:S(2)}) copy-start(f32[16,128,128]{2,1,0:T(8,128)} %all-reduce.6.cloned.1.call-done) | copy-start | bytes 3145732
  (6 other events, 6.7 us)
Sparse Core Ops, SparseCore 0:
  12.3 108.1 all-reduce.3
  164.6 103.9 all-reduce.5
where the time goes:
time: 294 us; the launch traced here: 292 us
  waiting for transfers between devices  152 us (52%)
  local copies, waits for them, and re-layouts  53.5 us (18%)
  matrix products  50 us (17%)
  between operations  15 us (5%)
  other arithmetic  13.6 us (5%)
  blocking collectives  8.75 us (3%)
    psum x1, waiting for transfers between devices, summed_prefix(): return lax.psum(partial_state, 'seq')  77.5 us
    psum x1, waiting for transfers between devices, body(): total_grad = lax.psum(grad_state, 'seq')  74.1 us
    unnamed x82, local copies, waits for them, and re-layouts  52 us
    psum x1, blocking collectives, body(): lax.psum((jnp.sum(attended * attended, axis=1), jnp.sum(scaled_cot * atte...  8.75 us
    dot_general x2, matrix products, intra_block(): jnp.einsum('hbs,she->bhe', scores, v_block, preferred_element_type=jnp.fl...  6.21 us
    dot_general x2, matrix products, backward_block(): jnp.einsum('bhe,hde->bhd', v_block, grad_bf, preferred_element_type=jnp.f...  6.01 us
  transfers between devices with their start and end apart: 2, of which 2 were waited for; matrix products, arithmetic and copies ran while one was open for 19% of the time, Pallas kernels for 0%

commit v1 on v0

--- a/solution.py
+++ b/solution.py
@@ -8,6 +8,14 @@
 HEAD_DIM = 128
 BLOCK = 256
 epsilon = 1e-06
+
+
+def add_in_pairs(x, mesh_axis):
+    size, total = (lax.axis_size(mesh_axis), x)
+    for reach in [1 << k for k in range(size.bit_length() - 1)]:
+        swap = [(i, i ^ reach) for i in range(size)]
+        total = total + lax.ppermute(total, mesh_axis, swap)
+    return total
 
 
 def summed_prefix(partial_state):
@@ -118,7 +126,7 @@
         key_parts.insert(0, packed[1])
         value_parts.insert(0, packed[2])
         grad_state = packed[3]
-    total_grad = lax.psum(grad_state, "seq")
+    total_grad = add_in_pairs(grad_state, "seq")
     wide_keys = pre_keys.astype(jnp.float32)
     wide_values = pre_values.astype(jnp.float32)
     prefix_key_grad = jnp.einsum(

time: 294 us -> 276 us (0.939)
  waiting for transfers between devices: 152 us -> 129 us
  starting transfers between devices: 0.08 us -> 9.88 us
  matrix products: 50 us -> 40.3 us
  other arithmetic: 13.6 us -> 17.6 us
    psum x1 -> x0, waiting for transfers between devices: 74.1 us -> none  [body(): total_grad = lax.psum(grad_state, 'seq')]
    ppermute x0 -> x5, waiting for transfers between devices: none -> 51.5 us  [add_in_pairs(): total = total + lax.ppermute(total, mesh_axis, swap)]
    ppermute x0 -> x5, starting transfers between devices: none -> 9.84 us  [add_in_pairs(): total = total + lax.ppermute(total, mesh_axis, swap)]
    dot_general x2, matrix products: 6.01 us -> 0.85 us  [backward_block(): jnp.einsum('bhe,hde->bhd', v_block, grad_bf, preferred_element_type=jnp.f...]
    add x0 -> x4, other arithmetic: none -> 4.02 us  [add_in_pairs(): total = total + lax.ppermute(total, mesh_axis, swap)]
    dot_general x2, matrix products: 4.79 us -> 0.94 us  [backward_block(): jnp.einsum('bhd,hde->bhe', k_block, grad_bf, preferred_element_type=jnp.f...]
    dot_general x2, matrix products: 0.89 us -> 3.85 us  [backward_block(): jnp.einsum('bhe,hde->bhd', d_block, state_bf, preferred_element_type=jnp....]
    unnamed x82 -> x80, local copies, waits for them, and re-layouts: 52 us -> 50.1 us
  transfers between devices with their start and end apart: 2 -> 6, of which waited for: 2 -> 6; matrix products, arithmetic and copies ran while one was open for 19% -> 23% of each run, Pallas kernels for 0% -> 0%
where the time goes in v1:
time: 276 us; the launch traced here: 272 us
  waiting for transfers between devices  129 us (47%)
  local copies, waits for them, and re-layouts  51.7 us (19%)
  matrix products  40.3 us (15%)
  other arithmetic  17.6 us (6%)
  between operations  15.1 us (5%)
  starting transfers between devices  9.88 us (4%)
  blocking collectives  8.56 us (3%)
    psum x1, waiting for transfers between devices, summed_prefix(): return lax.psum(partial_state, 'seq')  77.5 us
    ppermute x5, waiting for transfers between devices, add_in_pairs(): total = total + lax.ppermute(total, mesh_axis, swap)  51.5 us
    unnamed x80, local copies, waits for them, and re-layouts  50.1 us
    ppermute x5, starting transfers between devices, add_in_pairs(): total = total + lax.ppermute(total, mesh_axis, swap)  9.84 us
    psum x1, blocking collectives, body(): lax.psum((jnp.sum(attended * attended, axis=1), jnp.sum(scaled_cot * atte...  8.56 us
    dot_general x2, matrix products, intra_block(): jnp.einsum('hbs,she->bhe', scores, v_block, preferred_element_type=jnp.fl...  6.21 us
  transfers between devices with their start and end apart: 6, of which 6 were waited for; matrix products, arithmetic and copies ran while one was open for 23% of the time, Pallas kernels for 0%

profile of v1, /device:TPU:1, one launch (start us, length us, event | category | flops | bytes accessed | tf_op | source)
XLA Modules:
  0.0 272.1 jit_solution(11718967605328679909)
XLA Ops:
  8.8 3.4 %fusion.8 = f32[16,128,128]{2,1,0:T(8,128)} fusion(bf16[512,2048]{1,0:T(8,128)(2,1)S(1)} %copy-done, bf16[512,2048]{1,0:T(8,128)(2,1)} %param.12), kind=kOutput, calls=%fused_computation.18 | convolution fusion | flops 268435456 | bytes 5242880 | tf_op jit(solution)/shard_map/thd,the->hde/dot_general | solution.py:41
  12.9 3.9 %copy.49 = bf16[512,2048]{0,1:T(8,128)(2,1)} copy(bf16[512,2048]{1,0:T(8,128)(2,1)} %param.8) | data formatting | bytes 4194304 | tf_op args[0]
  16.8 3.9 %copy.53 = bf16[512,2048]{0,1:T(8,128)(2,1)} copy(bf16[512,2048]{1,0:T(8,128)(2,1)} %param.9) | data formatting | bytes 4194304 | tf_op args[1]
  20.8 3.9 %copy.52 = bf16[512,2048]{0,1:T(8,128)(2,1)} copy(bf16[512,2048]{1,0:T(8,128)(2,1)} %param.10) | data formatting | bytes 4194304 | tf_op args[2]
  24.7 3.3 %broadcast_multiply_fusion = (bf16[512,2048]{0,1:T(8,128)(2,1)S(1)}, bf16[512,2048]{0,1:T(8,128)(2,1)S(1)}, bf16[512,2048]{0,1:T(8,128)(2,1)S(1)}) fusion(bf16[512,2048]{0,1:T(8,128)(2,1)} %copy.53, bf16[512]{0:T(512)(128)(2,1)S(1)} %fusion.40, bf16[512,2048]{0,1:T(8,128)(2,1)} %copy.52, bf16[512,2048]{0,1:T(8,128)(2,1)} %copy.49), kind=kLoop, calls=%fused_computation.49 | loop fusion | flops 3145728 | bytes 12583936 | tf_op jit(solution)/shard_map/mul | solution.py:34
  30.8 2.2 fusion.47
  33.0 2.1 multiply_convert_fusion.2
  35.0 3.9 %copy.61 = bf16[512,2048]{0,1:T(8,128)(2,1)} copy(bf16[512,2048]{1,0:T(8,128)(2,1)} %param.11) | data formatting | bytes 4194304 | tf_op args[3]
  39.0 4.1 %fusion.48 = f32[16,128,256]{2,1,0:T(8,128)} fusion(bf16[256,16,128]{0,2,1:T(8,128)(2,1)} %bitcast.146, bf16[16,256,256]{2,1,0:T(8,128)(2,1)} %multiply_convert_fusion.2), kind=kOutput, calls=%fused_computation.74 | convolution fusion | flops 268435456 | bytes 5242880 | tf_op jit(solution)/shard_map/hbs,she->bhe/dot_general | solution.py:51
  43.0 77.5 %all-reduce.3.cloned.1.call-done = f32[16,128,128]{2,1,0:T(8,128)} async-done(((f32[16,128,128]{2,1,0:T(8,128)}), f32[16,128,128]{2,1,0:T(8,128)}) %all-reduce.3.cloned.1.call-update) | async-done | bytes 1048592 | tf_op jit(solution)/shard_map/psum | solution.py:22
  120.5 2.1 fusion.29
  128.5 8.6 %all-reduce = (f32[512]{0:T(512)S(1)}, f32[512]{0:T(512)S(1)}) all-reduce(f32[512]{0:T(512)S(1)} %get-tuple-element.22, f32[512]{0:T(512)S(1)} %fusion.2), channel_id=1, replica_groups=mesh['head'=4,'seq'=32] {'head'}, use_global_device_ids=true, to_apply=%region_2.0 | all-reduce | flops 1024 | bytes 8192 | tf_op jit(solution)/shard_map/psum | solution.py:80
  137.1 4.5 %fusion.5 = (bf16[512,2048]{0,1:T(8,128)(2,1)S(1)}, bf16[512,2048]{0,1:T(8,128)(2,1)}) fusion(f32[512,16,128]{0,2,1:T(8,128)} %copy-done.1, f32[512]{0:T(512)S(1)} %get-tuple-element.32, f32[512]{0:T(512)S(1)} %get-tuple-element.19, f32[512]{0:T(512)S(1)} %get-tuple-element.33, f32[2048]{0:T(1024)S(1)} %copy-done.34, bf16[512,2048]{0,1:T(8,128)(2,1)} %copy.61, ...), kind=kLoop, calls=%fused_computation.9 | loop fusion | flops 11534336 | bytes 10501120 | tf_op jit(solution)/shard_map/convert_element_type | solution.py:87
  144.1 2.8 %collective-permute-start = (f32[16,128,128]{2,1,0:T(8,128)S(1)}, f32[16,128,128]{2,1,0:T(8,128)S(1)}, u32[]{:S(2)}, u32[]{:S(2)}) collective-permute-start(f32[16,128,128]{2,1,0:T(8,128)S(1)} %convolution_add_fusion), channel_id=1, source_target_pairs={{0,1},{1,0},{2,3},{3,2},{4,5},{5,4},{6,7},{7,6},{8,9},{9,8},{10,11... | collective-permute-start | bytes 3145736 | tf_op jit(solution)/shard_map/ppermute | solution.py:17
  153.5 19.8 %collective-permute-done.1 = f32[16,128,128]{2,1,0:T(8,128)S(1)} collective-permute-done((f32[16,128,128]{2,1,0:T(8,128)S(1)}, f32[16,128,128]{2,1,0:T(8,128)S(1)}, u32[]{:S(2)}, u32[]{:S(2)}) %collective-permute-start.1) | collective-permute-done | bytes 1048608 | tf_op jit(solution)/shard_map/ppermute | solution.py:17
  173.5 2.7 collective-permute-start.2
  178.3 2.1 fusion.49
  180.4 17.5 %collective-permute-done.2 = f32[16,128,128]{2,1,0:T(8,128)S(1)} collective-permute-done((f32[16,128,128]{2,1,0:T(8,128)S(1)}, f32[16,128,128]{2,1,0:T(8,128)S(1)}, u32[]{:S(2)}, u32[]{:S(2)}) %collective-permute-start.2) | collective-permute-done | bytes 1048608 | tf_op jit(solution)/shard_map/ppermute | solution.py:17
  201.5 4.0 %copy.82 = bf16[512,2048]{1,0:T(8,128)(2,1)} copy(bf16[512,2048]{0,1:T(8,128)(2,1)} %bitcast.151) | data formatting | bytes 4194304
  205.5 2.4 fusion.23
  209.5 4.0 %copy.80 = bf16[512,2048]{1,0:T(8,128)(2,1)} copy(bf16[512,2048]{0,1:T(8,128)(2,1)} %bitcast.152) | data formatting | bytes 4194304
  213.5 2.0 fusion.53
  215.5 5.7 %collective-permute-done.3 = f32[16,128,128]{2,1,0:T(8,128)} collective-permute-done((f32[16,128,128]{2,1,0:T(8,128)}, f32[16,128,128]{2,1,0:T(8,128)}, u32[]{:S(2)}, u32[]{:S(2)}) %collective-permute-start.3) | collective-permute-done | bytes 1048608 | tf_op jit(solution)/shard_map/ppermute | solution.py:17
  221.3 2.7 add.86
  223.9 3.2 %collective-permute-start.4 = (f32[16,128,128]{2,1,0:T(8,128)}, f32[16,128,128]{2,1,0:T(8,128)}, u32[]{:S(2)}, u32[]{:S(2)}) collective-permute-start(f32[16,128,128]{2,1,0:T(8,128)} %add.86), channel_id=1, source_target_pairs={{0,16},{1,17},{2,18},{3,19},{4,20},{5,21},{6,22},{7,23},{8,24},{9,... | collective-permute-start | bytes 3145736 | tf_op jit(solution)/shard_map/ppermute | solution.py:17
  231.1 3.9 %copy.81 = bf16[512,2048]{1,0:T(8,128)(2,1)} copy(bf16[512,2048]{0,1:T(8,128)(2,1)} %bitcast.153) | data formatting | bytes 4194304
  235.0 3.9 %copy.79 = bf16[512,2048]{1,0:T(8,128)(2,1)} copy(bf16[512,2048]{0,1:T(8,128)(2,1)} %get-tuple-element.21) | data formatting | bytes 4194304
  238.9 8.3 %collective-permute-done.4 = f32[16,128,128]{2,1,0:T(8,128)} collective-permute-done((f32[16,128,128]{2,1,0:T(8,128)}, f32[16,128,128]{2,1,0:T(8,128)}, u32[]{:S(2)}, u32[]{:S(2)}) %collective-permute-start.4) | collective-permute-done | bytes 1048608 | tf_op jit(solution)/shard_map/ppermute | solution.py:17
  247.2 4.7 %fusion.16 = bf16[16,128,512]{2,1,0:T(8,128)(2,1)} fusion(f32[16,128,128]{2,1,0:T(8,128)} %add.86, f32[16,128,128]{2,1,0:T(8,128)} %collective-permute-done.4, bf16[512,2048]{1,0:T(8,128)(2,1)S(1)} %copy-done), kind=kOutput, calls=%fused_computation.35 | convolution fusion | flops 1611923456 | bytes 6291456 | tf_op jit(solution)/shard_map/the,hde->thd/dot_general | solution.py:132
  252.0 3.9 %copy.83 = bf16[512,2048]{1,0:T(8,128)(2,1)} copy(bf16[512,2048]{0,1:T(8,128)(2,1)} %bitcast.150) | data formatting | bytes 4194304
  255.9 5.5 %fusion.13 = bf16[16,128,512]{2,1,0:T(8,128)(2,1)} fusion(f32[16,128,128]{2,1,0:T(8,128)} %add.86, f32[16,128,128]{2,1,0:T(8,128)} %collective-permute-done.4, bf16[512,2048]{1,0:T(8,128)(2,1)} %param.12), kind=kOutput, calls=%fused_computation.34 | convolution fusion | flops 1611923456 | bytes 6291456 | tf_op jit(solution)/shard_map/thd,hde->the/dot_general | solution.py:135
  261.4 3.9 %copy.84 = bf16[512,2048]{1,0:T(8,128)(2,1)} copy(bf16[512,2048]{0,1:T(8,128)(2,1)} %bitcast.149) | data formatting | bytes 4194304
  (105 shorter events, 30.6 us)
Async XLA Ops:
  7.2 1.6 copy-start
  7.2 113.4 %all-reduce.3.cloned.1.call-start = ((), (), s32[]{:S(2)}) async-start(), calls=%async_computation | async-start | bytes 2097152 | tf_op jit(solution)/shard_map/psum | solution.py:22
  28.1 4.9 %copy-start.24 = (bf16[256,2048]{0,1:T(8,128)(2,1)}, bf16[256,2048]{0,1:T(8,128)(2,1)S(1)}, u32[]{:S(2)}) copy-start(bf16[256,2048]{0,1:T(8,128)(2,1)S(1)} %get-tuple-element.31) | copy-start | bytes 3145732
  29.5 3.5 %copy-start.7 = (bf16[256,2048]{0,1:T(8,128)(2,1)}, bf16[256,2048]{0,1:T(8,128)(2,1)S(1)}, u32[]{:S(2)}) copy-start(bf16[256,2048]{0,1:T(8,128)(2,1)S(1)} %get-tuple-element.27) | copy-start | bytes 3145732
  30.4 2.5 copy-start.16
  120.5 2.1 copy-start.8
  120.5 2.5 copy-start.30
  123.1 1.7 copy-start.28
  123.1 2.4 copy-start.29
  126.0 1.7 copy-start.15
  126.0 1.7 copy-start.34
  126.6 2.0 copy-start.1
  141.6 1.6 copy-start.9
  141.7 34.4 %copy-start.5 = (bf16[256,2048]{0,1:T(8,128)(2,1)}, bf16[256,2048]{0,1:T(8,128)(2,1)S(1)}, u32[]{:S(2)}) copy-start(bf16[256,2048]{0,1:T(8,128)(2,1)S(1)} %get-tuple-element.24) | copy-start | bytes 3145732
  141.7 1.9 copy-start.13
  143.6 33.3 %copy-start.22 = (f32[16,128,128]{2,1,0:T(8,128)}, f32[16,128,128]{2,1,0:T(8,128)S(1)}, u32[]{:S(2)}) copy-start(f32[16,128,128]{2,1,0:T(8,128)S(1)} %fusion.51) | copy-start | bytes 3145732
  143.7 3.2 %copy-start.26 = (bf16[256,2048]{0,1:T(8,128)(2,1)S(1)}, bf16[256,2048]{0,1:T(8,128)(2,1)}, u32[]{:S(2)}) copy-start(bf16[256,2048]{0,1:T(8,128)(2,1)} %get-tuple-element.37) | copy-start | bytes 3145732
  144.1 3.6 %copy-start.25 = (bf16[256,2048]{0,1:T(8,128)(2,1)S(1)}, bf16[256,2048]{0,1:T(8,128)(2,1)}, u32[]{:S(2)}) copy-start(bf16[256,2048]{0,1:T(8,128)(2,1)} %copy-done.24) | copy-start | bytes 3145732
  144.1 5.0 %collective-permute-start = (f32[16,128,128]{2,1,0:T(8,128)S(1)}, f32[16,128,128]{2,1,0:T(8,128)S(1)}, u32[]{:S(2)}, u32[]{:S(2)}) collective-permute-start(f32[16,128,128]{2,1,0:T(8,128)S(1)} %convolution_add_fusion), channel_id=1, source_target_pairs={{0,1},{1,0},{2,3},{3,2},{4,5},{5,4},{6,7},{7,6},{8,9},{9,8},{10,11... | collective-permute-start | bytes 3145736 | tf_op jit(solution)/shard_map/ppermute | solution.py:17
  149.3 2.2 copy-start.18
  149.3 24.0 %collective-permute-start.1 = (f32[16,128,128]{2,1,0:T(8,128)S(1)}, f32[16,128,128]{2,1,0:T(8,128)S(1)}, u32[]{:S(2)}, u32[]{:S(2)}) collective-permute-start(f32[16,128,128]{2,1,0:T(8,128)S(1)} %add.83), channel_id=1, source_target_pairs={{0,2},{1,3},{2,0},{3,1},{4,6},{5,7},{6,4},{7,5},{8,10},{9,11},{10,... | collective-permute-start | bytes 3145736 | tf_op jit(solution)/shard_map/ppermute | solution.py:17
  151.5 1.6 copy-start.17
  153.5 22.6 %copy-start.3 = (bf16[256,2048]{0,1:T(8,128)(2,1)S(1)}, bf16[256,2048]{0,1:T(8,128)(2,1)}, u32[]{:S(2)}) copy-start(bf16[256,2048]{0,1:T(8,128)(2,1)} %copy-done.2) | copy-start | bytes 3145732
  173.5 24.4 %collective-permute-start.2 = (f32[16,128,128]{2,1,0:T(8,128)S(1)}, f32[16,128,128]{2,1,0:T(8,128)S(1)}, u32[]{:S(2)}, u32[]{:S(2)}) collective-permute-start(f32[16,128,128]{2,1,0:T(8,128)S(1)} %add.84), channel_id=1, source_target_pairs={{0,4},{1,5},{2,6},{3,7},{4,0},{5,1},{6,2},{7,3},{8,12},{9,13},{10,... | collective-permute-start | bytes 3145736 | tf_op jit(solution)/shard_map/ppermute | solution.py:17
  199.0 22.2 %collective-permute-start.3 = (f32[16,128,128]{2,1,0:T(8,128)}, f32[16,128,128]{2,1,0:T(8,128)}, u32[]{:S(2)}, u32[]{:S(2)}) collective-permute-start(f32[16,128,128]{2,1,0:T(8,128)} %add.85), channel_id=1, source_target_pairs={{0,8},{1,9},{2,10},{3,11},{4,12},{5,13},{6,14},{7,15},{8,0},{9,1},... | collective-permute-start | bytes 3145736 | tf_op jit(solution)/shard_map/ppermute | solution.py:17
  201.5 4.0 %copy-start.6 = (bf16[256,2048]{0,1:T(8,128)(2,1)S(1)}, bf16[256,2048]{0,1:T(8,128)(2,1)}, u32[]{:S(2)}) copy-start(bf16[256,2048]{0,1:T(8,128)(2,1)} %copy-done.5) | copy-start | bytes 3145732
  205.5 2.4 copy-start.33
  209.5 4.0 %copy-start.10 = (bf16[256,2048]{0,1:T(8,128)(2,1)S(1)}, bf16[256,2048]{0,1:T(8,128)(2,1)}, u32[]{:S(2)}) copy-start(bf16[256,2048]{0,1:T(8,128)(2,1)} %copy-done.7) | copy-start | bytes 3145732
  215.5 11.6 %copy-start.27 = (bf16[256,2048]{0,1:T(8,128)(2,1)S(1)}, bf16[256,2048]{0,1:T(8,128)(2,1)}, u32[]{:S(2)}) copy-start(bf16[256,2048]{0,1:T(8,128)(2,1)} %get-tuple-element.37) | copy-start | bytes 3145732
  223.9 3.6 %copy-start.14 = (bf16[256,2048]{0,1:T(8,128)(2,1)S(1)}, bf16[256,2048]{0,1:T(8,128)(2,1)}, u32[]{:S(2)}) copy-start(bf16[256,2048]{0,1:T(8,128)(2,1)} %copy-done.11) | copy-start | bytes 3145732
  223.9 3.7 %copy-start.21 = (bf16[16,256,256]{2,1,0:T(8,128)(2,1)S(1)}, bf16[16,256,256]{2,1,0:T(8,128)(2,1)}, u32[]{:S(2)}) copy-start(bf16[16,256,256]{2,1,0:T(8,128)(2,1)} %copy-done.20) | copy-start | bytes 6291460
  223.9 23.3 %collective-permute-start.4 = (f32[16,128,128]{2,1,0:T(8,128)}, f32[16,128,128]{2,1,0:T(8,128)}, u32[]{:S(2)}, u32[]{:S(2)}) collective-permute-start(f32[16,128,128]{2,1,0:T(8,128)} %add.86), channel_id=1, source_target_pairs={{0,16},{1,17},{2,18},{3,19},{4,20},{5,21},{6,22},{7,23},{8,24},{9,... | collective-permute-start | bytes 3145736 | tf_op jit(solution)/shard_map/ppermute | solution.py:17
  (9 other events, 10.9 us)
Sparse Core Ops, SparseCore 0:
  12.4 108.1 all-reduce.2
